TPU v7x, 32 devices: a whole 2x2x4 slice. The times are simulated.
32 devices in a mesh: wide: 16 (over z, y, core), narrow: 2 (over x).
Axes of the slice: x: 2, y: 2, z: 4, core: 2. Of those that a mesh axis runs over, the one named last changes fastest.
Arguments:
- state: bfloat16 [2, 4194304], P(None, ('wide', 'narrow')), may hold values from -6 to 6
- blocks_one: bfloat16 [16, 2, 512, 512], P('wide'), may hold values from -0.1875 to 0.1875
- blocks_two: bfloat16 [16, 2, 512, 512], P('wide'), may hold values from -0.1875 to 0.1875
- control_of: int32 [16], replicated, may hold values from 0 to 15, each once
- ctrl_qubits: int32 [4], replicated, may hold values from 9 to 16, as said below
- angles: float32 [3], replicated, may hold values from -3.140625 to 3.140625
Outputs:
- final_state: float32 [2, 4194304], P(None, ('wide', 'narrow'))
Inputs may be any that keep to these rules, and one draw needn't show every extreme that they name: `ctrl_qubits`: distinct local qubits, none of them among the lowest 9; the lowest and the highest allowed qubit are always among them.
All inputs are finite; a program needn't handle non-finite values.
Results may differ from a plain program's by a relative error of at most 0.0041.
Values may be sent and summed in bfloat16 or wider, within the bound.
A program may use at most 64 MiB of HBM per device.

v0:
```python
import jax
import jax.numpy as jnp
from jax import lax
from jax.sharding import PartitionSpec as P


def swapped(value, axis, apart):
    mask = 2**apart
    pairs = [(source, source ^ mask) for source in range(lax.axis_size(axis))]
    return lax.ppermute(value, axis, pairs)


def slot_index(ctrl_qubits, control_of, local_bits, low_count, high_count):
    slot_count = control_of.shape[0]
    qubit_ids = jnp.arange(local_bits, dtype=jnp.int32)
    matches = ctrl_qubits[:, None] == qubit_ids[None, :]
    control_mask = jnp.any(matches, axis=0)
    place_ids = jnp.arange(ctrl_qubits.shape[0], dtype=jnp.int32)
    control_place = jnp.sum(jnp.where(matches, place_ids[:, None], 0), axis=0)
    rest_rank = jnp.cumsum(1 - control_mask.astype(jnp.int32)) - 1
    values = control_of.reshape(slot_count, 1, 1)
    low_ids = jnp.arange(low_count, dtype=jnp.int32).reshape(1, low_count, 1)
    high_ids = jnp.arange(high_count, dtype=jnp.int32).reshape(1, 1, high_count)
    rest_index = low_ids + low_count * high_ids
    result = jnp.zeros((slot_count, low_count, high_count), jnp.int32)
    for qubit in range(local_bits):
        from_control = jnp.right_shift(values, control_place[qubit]) & 1
        from_rest = jnp.right_shift(rest_index, jnp.maximum(rest_rank[qubit], 0)) & 1
        chosen_bit = jnp.where(control_mask[qubit], from_control, from_rest)
        result = result + jnp.left_shift(chosen_bit, qubit)
    return result


def complex_rows(field, weights):
    products = jnp.einsum("crs,dst->cdrt", field, weights, preferred_element_type=jnp.float32)
    return jnp.stack([products[0, 0] - products[1, 1], products[0, 1] + products[1, 0]])


def complex_cols(field, weights):
    products = jnp.einsum("cth,dtu->cduh", field, weights, preferred_element_type=jnp.float32)
    return jnp.stack([products[0, 0] - products[1, 1], products[0, 1] + products[1, 0]])


def rotate(field, angles):
    top_bit = lax.axis_size("narrow").bit_length() - 2
    partner = swapped(field, "narrow", top_bit).astype(jnp.float32)
    own_field = field.astype(jnp.float32)
    polar = angles[0] * 0.5
    first_angle = angles[1]
    third_angle = angles[2]
    cosine = jnp.cos(polar)
    sine = jnp.sin(polar)
    upper = jnp.right_shift(lax.axis_index("narrow"), top_bit) & 1 == 1
    own_re = jnp.where(upper, jnp.cos(first_angle + third_angle) * cosine, cosine)
    own_im = jnp.where(upper, jnp.sin(first_angle + third_angle) * cosine, 0.0)
    other_re = jnp.where(upper, jnp.cos(first_angle) * sine, -jnp.cos(third_angle) * sine)
    other_im = jnp.where(upper, jnp.sin(first_angle) * sine, -jnp.sin(third_angle) * sine)
    new_re = (
        own_re * own_field[0]
        - own_im * own_field[1]
        + other_re * partner[0]
        - other_im * partner[1]
    )
    new_im = (
        own_re * own_field[1]
        + own_im * own_field[0]
        + other_re * partner[1]
        + other_im * partner[0]
    )
    return jnp.stack([new_re, new_im])


def send_back(mixed):
    return lax.all_to_all(mixed, "wide", split_axis=2, concat_axis=1, tiled=True)


def shards(state, blocks_one, blocks_two, control_of, ctrl_qubits, angles):
    local_count = state.shape[1]
    order = blocks_one.shape[2]
    slot_count = lax.axis_size("wide")
    low_count = order // slot_count
    high_count = local_count // order
    rows_per_slot = high_count // slot_count
    local_bits = local_count.bit_length() - 1
    target_bits = order.bit_length() - 1
    rotated = rotate(state, angles).astype(jnp.bfloat16)
    rows_first = rotated.reshape(2, high_count, order)
    first = complex_rows(rows_first, blocks_one[0]).astype(jnp.bfloat16)
    row_ids = slot_index(
        ctrl_qubits - target_bits, control_of, local_bits - target_bits, 1, rows_per_slot
    ).reshape(-1)
    picked = jnp.take(first, row_ids, axis=1).reshape(
        2, slot_count, rows_per_slot, slot_count, low_count
    )
    arranged = jnp.transpose(picked, (0, 1, 4, 2, 3)).reshape(2, slot_count, low_count, high_count)
    received = lax.all_to_all(arranged, "wide", split_axis=1, concat_axis=2, tiled=True)
    mixed = complex_cols(received[:, 0], blocks_two[0])[:, None]
    returned = send_back(mixed)
    back_rows = returned.reshape(2, slot_count, low_count, rows_per_slot, slot_count)
    back_rows = jnp.transpose(back_rows, (0, 1, 3, 4, 2)).reshape(2, high_count, order)
    restored = jnp.zeros((2, high_count, order), jnp.float32).at[:, row_ids].set(back_rows)
    return restored.reshape(2, local_count)


def solution(mesh):
    in_specs = (
        P(None, ("wide", "narrow")),
        P("wide", None, None, None),
        P("wide", None, None, None),
        P(),
        P(),
        P(),
    )
    out_specs = P(None, ("wide", "narrow"))
    return jax.shard_map(shards, mesh=mesh, in_specs=in_specs, out_specs=out_specs, check_vma=False)
```

profile of v0, /device:TPU:0, one launch (start us, length us, event | category | flops | bytes accessed | tf_op | source)
XLA Modules:
  0.0 124.5 jit_solution(7495916964244648954)
XLA Ops:
  0.0 0.0 copy-start
  0.0 2.9 %collective-permute-start = (bf16[2,131072]{1,0:T(2,128)(2,1)}, bf16[2,131072]{1,0:T(2,128)(2,1)S(1)}, u32[]{:S(2)}, u32[]{:S(2)}) collective-permute-start(bf16[2,131072]{1,0:T(2,128)(2,1)} %param.6), channel_id=1, source_target_pairs={{0,1},{1,0},{2,3},{3,2},{4,5},{5,4},{6,7},{7,6},{8,9},{9,8},{10,11... | collective-permute-start | bytes 1572872 | tf_op jit(solution)/shard_map/ppermute | solution.py:10
  2.9 1.4 %fusion.12 = (f32[1]{0:T(128)}, f32[1]{0:T(128)}, f32[1]{0:T(128)}) fusion(f32[3]{0:T(128)} %param.11), kind=kLoop, calls=%fused_computation.52 | loop fusion | bytes 24 | tf_op jit(solution)/shard_map/slice | solution.py:50
  9.5 1.4 %convert_element_type.21 = f32[2,131072]{1,0:T(2,128)S(1)} convert(bf16[2,131072]{1,0:T(2,128)(2,1)} %param.6) | non-fusion elementwise | flops 262144 | bytes 1572864 | tf_op jit(solution)/shard_map/convert_element_type | solution.py:47
  11.0 0.7 broadcast_add_fusion.1
  11.6 0.1 select_reduce_fusion
  11.7 0.1 fusion.10
  11.8 0.7 fusion.13
  12.5 0.7 fusion.14
  13.2 0.2 reduce-window.9
  13.4 0.7 fusion.15
  19.1 5.7 %shift-right-arithmetic_and_fusion.15 = (s32[16]{0:T(128)S(1)}, s32[16]{0:T(128)S(1)}, s32[16]{0:T(128)S(1)}, s32[16]{0:T(128)S(1)}, s32[16]{0:T(128)S(1)}, /*in...) fusion(s32[16]{0:T(128)} %param.9, s32[]{:T(128)} %bitcast.1, s32[]{:T(128)} %bitcast.17, s32[]{:T(128)} %bitcast.14, ...), kind=kLoop, calls=%fused_computation.48 | loop fusion | flops 256 | bytes 608 | tf_op jit(solution)/shard_map/and | solution.py:27
  24.8 5.1 %add_add_fusion = s32[16,1,1,16]{3,0,2,1:T(8,128)S(1)} fusion(s32[16]{0:T(128)S(1)} %get-tuple-element.46, s32[16]{0:T(128)S(1)} %get-tuple-element.28, s32[16]{0:T(128)S(1)} %get-tuple-element.47, s32[16]{0:T(128)S(1)} %get-tuple-element.29, s32[16]{0:T(128)S(1)} %get-tuple-element.48, s32[16]{0:T(128)S(1)} %get-tuple-element.23, ...), kind=kLoop, calls=%fused_computation.25 | loop fusion | flops 5888 | bytes 2056 | tf_op jit(solution)/shard_map/add | solution.py:30
  29.8 0.1 reshape.711
  29.9 5.1 %compare_and_fusion = pred[16,16]{1,0:T(8,128)(4,1)S(1)} fusion(s32[16]{0:T(128)S(1)} %get-tuple-element.46, s32[16]{0:T(128)S(1)} %get-tuple-element.28, s32[16]{0:T(128)S(1)} %get-tuple-element.47, s32[16]{0:T(128)S(1)} %get-tuple-element.29, s32[16]{0:T(128)S(1)} %get-tuple-element.48, s32[16]{0:T(128)S(1)} %get-tuple-element.23, ...), kind=kLoop, calls=%fused_computation.26 | loop fusion | flops 7424 | bytes 1288 | tf_op jit(solution)/shard_map/jit(_take)/and | solution.py:92
  35.0 0.0 collective-permute-done
  35.0 0.4 convert_element_type.22
  35.4 5.6 %convert_reduce_fusion.1 = (bf16[131072]{0:T(1024)(128)(2,1)S(1)}, bf16[131072]{0:T(1024)(128)(2,1)S(1)}) fusion(f32[2,131072]{1,0:T(2,128)S(1)} %convert_element_type.22, f32[2,131072]{1,0:T(2,128)S(1)} %convert_element_type.21, f32[]{:T(128)S(6)} %select_n.273, f32[]{:T(128)S(6)} %select_n.272, f32[]{:T(128)S(6)} %select_n.271, f32[]{:T(128)S(6)} %select_n.270), kind=kLoop, calls=%fused_computation.21 | loop fusion | flops 2097152 | bytes 2621456 | tf_op jit(solution)/shard_map/convert.7
  41.0 0.2 stack.20
  41.1 0.2 stack.21
  41.3 0.0 copy-done
  41.3 0.7 convolution_bitcast_fusion.1
  42.0 0.2 fusion.8
  42.2 0.1 pad_maximum_fusion
  42.2 0.5 copy.50
  42.8 2.5 %gather_fusion = bf16[256,2,512]{2,1,0:T(2,128)(2,1)} fusion(bf16[2,256,512]{2,0,1:T(2,128)(2,1)S(1)} %copy.50, s32[1024]{0:T(1024)S(1)} %pad_clamp_fusion), kind=kCustom, calls=%fused_computation | custom fusion | bytes 1049600 | tf_op jit(solution)/shard_map/jit(_take)/gather | solution.py:92
  45.3 3.0 %gather.7 = bf16[2,16,16,16,32]{4,3,0,2,1:T(8,128)(2,1)S(1)} reshape(bf16[2,256,512]{2,0,1:T(2,128)(2,1)} %bitcast.89) | data formatting | bytes 1048576 | tf_op jit(solution)/shard_map/jit(_take)/gather | solution.py:92
  48.3 1.6 %copy_select_fusion = bf16[2,16,16,16,32]{4,3,2,1,0:T(8,128)(2,1)} fusion(bf16[2,16,16,16,32]{4,3,0,2,1:T(8,128)(2,1)S(1)} %gather.7, pred[16,16]{1,0:T(8,128)(4,1)S(1)} %compare_and_fusion), kind=kLoop, calls=%fused_computation.2 | loop fusion | flops 262144 | bytes 1048832 | tf_op jit(solution)/shard_map/jit(_take)/select_n | solution.py:92
  49.8 0.0 copy-start.2
  49.8 2.0 %copy.52 = bf16[2,16,32,256]{3,2,0,1:T(8,128)(2,1)S(1)} copy(bf16[2,16,32,256]{2,3,1,0:T(8,128)(2,1)} %bitcast.87) | data formatting | bytes 1048576 | tf_op jit(solution)/shard_map/reshape | solution.py:95
  51.8 20.2 %all_to_all.8 = bf16[2,16,32,256]{3,2,0,1:T(8,128)(2,1)S(1)} all-to-all(bf16[2,16,32,256]{3,2,0,1:T(8,128)(2,1)S(1)} %copy.52), channel_id=1, replica_groups=mesh['wide'=16,'narrow'=2] {'wide'}, dimensions={1} | all-to-all | bytes 1048576 | tf_op jit(solution)/shard_map/all_to_all | solution.py:96
  72.1 0.0 copy-done.2
  72.1 0.7 convolution_bitcast_fusion
  72.8 0.2 fusion.3
  73.0 0.1 maximum_bitcast_fusion
  73.1 0.6 copy.55
  73.7 28.9 %all_to_all.9 = f32[2,1,512,256]{3,0,1,2:T(2,128)} all-to-all(f32[2,1,512,256]{3,0,1,2:T(2,128)S(1)} %copy.55), channel_id=1, replica_groups=mesh['wide'=16,'narrow'=2] {'wide'}, dimensions={2} | all-to-all | bytes 2097152 | tf_op jit(solution)/shard_map/all_to_all | solution.py:74
  102.5 1.5 %copy.56 = f32[2,1,512,256]{2,3,0,1:T(8,128)S(1)} copy(f32[2,1,512,256]{3,0,1,2:T(2,128)} %all_to_all.9) | data formatting | bytes 2097152 | tf_op jit(solution)/shard_map/all_to_all | solution.py:74
  104.0 2.5 %reshape.688 = f32[2,16,32,16,16]{2,1,4,3,0:T(8,128)} reshape(f32[2,1,512,256]{2,3,0,1:T(8,128)S(1)} %copy.56) | data formatting | bytes 2097152 | tf_op jit(solution)/shard_map/reshape | solution.py:99
  106.5 5.4 %copy.57 = f32[2,16,16,16,32]{4,3,2,1,0:T(8,128)} copy(f32[2,16,16,16,32]{4,1,3,2,0:T(8,128)} %bitcast.86) | data formatting | bytes 2097152 | tf_op jit(solution)/shard_map/transpose | solution.py:100
  111.9 3.5 %reshape.704 = f32[2,256,512]{2,1,0:T(8,128)S(1)} reshape(f32[2,16,16,16,32]{4,3,2,1,0:T(8,128)} %copy.57) | data formatting | bytes 2097152 | tf_op jit(solution)/shard_map/reshape | solution.py:100
  115.5 0.8 copy.58
  116.3 0.3 broadcast_in_dim.150
  116.6 6.9 %scatter_fusion = f32[2,256,512]{2,0,1:T(2,128)S(1)} fusion(f32[2,256,512]{2,0,1:T(2,128)S(1)} %broadcast_in_dim.150, s32[256]{0:T(256)S(1)} %bitcast.92, f32[256,2,512]{2,1,0:T(2,128)S(1)} %copy.58), kind=kCustom, calls=%fused_computation.1 | custom fusion | bytes 3146752 | tf_op jit(solution)/shard_map/scatter | solution.py:101
  123.5 0.0 copy-start.1
  123.5 1.0 copy-done.1
  (9 shorter events, 0.1 us)
Async XLA Ops:
  0.0 41.3 %copy-start = (bf16[1,2,512,512]{3,2,1,0:T(8,128)(2,1)S(1)}, bf16[1,2,512,512]{3,2,1,0:T(8,128)(2,1)}, u32[]{:S(2)}) copy-start(bf16[1,2,512,512]{3,2,1,0:T(8,128)(2,1)} %param.7) | copy-start | bytes 3145732
  0.0 35.0 %collective-permute-start = (bf16[2,131072]{1,0:T(2,128)(2,1)}, bf16[2,131072]{1,0:T(2,128)(2,1)S(1)}, u32[]{:S(2)}, u32[]{:S(2)}) collective-permute-start(bf16[2,131072]{1,0:T(2,128)(2,1)} %param.6), channel_id=1, source_target_pairs={{0,1},{1,0},{2,3},{3,2},{4,5},{5,4},{6,7},{7,6},{8,9},{9,8},{10,11... | collective-permute-start | bytes 1572872 | tf_op jit(solution)/shard_map/ppermute | solution.py:10
  49.8 22.2 %copy-start.2 = (bf16[1,2,512,512]{3,2,1,0:T(8,128)(2,1)S(1)}, bf16[1,2,512,512]{3,2,1,0:T(8,128)(2,1)}, u32[]{:S(2)}) copy-start(bf16[1,2,512,512]{3,2,1,0:T(8,128)(2,1)} %param.8) | copy-start | bytes 3145732
  123.5 1.0 copy-start.1
where the time goes:
time: 126 us; the launch traced here: 124 us
  blocking collectives  49.1 us (39%)
  local copies, waits for them, and re-layouts  34.4 us (27%)
  other arithmetic  26.2 us (21%)
  between operations  10.4 us (8%)
  starting transfers between devices  2.94 us (2%)
  matrix products  1.43 us (1%)
    all_to_all x1, blocking collectives, send_back(): lax.all_to_all(mixed, 'wide', split_axis=2, concat_axis=1, tiled=True)  28.9 us
    all_to_all x1, blocking collectives, shards(): lax.all_to_all(arranged, 'wide', split_axis=1, concat_axis=2, tiled=True)  20.2 us
    scatter x1, local copies, waits for them, and re-layouts, shards(): jnp.zeros((2, high_count, order), jnp.float32).at[:, row_ids].set(back_rows)  6.93 us
    another operation x2, other arithmetic  5.74 us
    and x1, other arithmetic, slot_index(): from_control = jnp.right_shift(values, control_place[qubit]) & 1  5.66 us
    gather x2, local copies, waits for them, and re-layouts, shards(): jnp.take(first, row_ids, axis=1)  5.47 us
    transpose x1, local copies, waits for them, and re-layouts, shards(): jnp.transpose(back_rows, (0, 1, 3, 4, 2)).reshape(2, high_count, order)  5.4 us
    and x1, other arithmetic, shards(): jnp.take(first, row_ids, axis=1)  5.07 us
  transfers between devices with their start and end apart: 1, of which 0 were waited for; matrix products, arithmetic and copies ran while one was open for 18% of the time, Pallas kernels for 0%

commit v1 on v0

v1 whole, which is shorter than its diff:
```python
import functools

import jax
import jax.numpy as jnp
from jax import lax
from jax.experimental import pallas as pl
from jax.experimental.pallas import tpu as pltpu
from jax.sharding import PartitionSpec as P

LANES = 128
F32 = jnp.float32
BF16 = jnp.bfloat16
MESH = pl.DeviceIdType.MESH


def dot(a, b):
    return jnp.dot(a, b, preferred_element_type=F32)


def slot_and_rank(rows, row_bits, target_bits, ctrl, control_of):
    value = jnp.zeros_like(rows)
    rank = jnp.zeros_like(rows)
    free = jnp.int32(1)
    for bit in range(row_bits):
        here = (rows >> bit) & 1
        weight = jnp.int32(0)
        taken = jnp.int32(0)
        for place, qubit in enumerate(ctrl):
            match = (qubit == bit + target_bits).astype(jnp.int32)
            weight = weight + match * (1 << place)
            taken = taken + match
        value = value + here * weight
        rank = rank + here * (free * (1 - taken))
        free = free * (2 - taken)
    slot = jnp.zeros_like(rows)
    for index, acts_at in enumerate(control_of):
        slot = slot + jnp.where(value == acts_at, index, 0)
    return slot, rank


def coefficients(cosine, sine, upper):
    own_re = jnp.where(upper, cosine[3] * cosine[0], cosine[0])
    own_im = jnp.where(upper, sine[3] * cosine[0], jnp.zeros_like(sine[3]))
    other_re = jnp.where(upper, cosine[1] * sine[0], -cosine[2] * sine[0])
    other_im = jnp.where(upper, sine[1] * sine[0], -sine[2] * sine[0])
    return own_re, own_im, other_re, other_im


def combine(coefs, own_re, own_im, far_re, far_im):
    a, b, c, d = coefs
    return (
        a * own_re - b * own_im + c * far_re - d * far_im,
        a * own_im + b * own_re + c * far_im + d * far_re,
    )


def kernel(
    dims,
    ctrl_ref, cof_ref, ang_ref, x_ref, w1_ref, w2_ref,
    out_ref,
    x32, xs, own, part, rot, wraw, wc1, wc2, perm, back,
    send, recv, xmat, ymat, ysend, ret, rmat,
    load_sem, swap_send, swap_recv, go_send, go_recv, ret_send, ret_recv,
):
    slots, n_narrow, order, rows, phases, low = dims
    slot_rows = rows // slots
    h = slot_rows // phases
    part_rows = rows // phases
    tiles = order // LANES
    group = LANES // low
    v_his = slots // group
    qh = tiles * h
    target_bits = order.bit_length() - 1
    me = lax.axis_index("wide")
    mine = lax.axis_index("narrow")
    partner = lax.rem(mine + n_narrow // 2, n_narrow)

    loads = [
        pltpu.make_async_copy(w_ref.at[0], wraw.at[i], load_sem.at[i])
        for i, w_ref in enumerate((w1_ref, w2_ref))
    ]
    for load in loads:
        load.start()

    barrier = pltpu.get_barrier_semaphore()
    for k in range(1, slots):
        pl.semaphore_signal(barrier, inc=1, device_id=(lax.rem(me + k, slots), mine), device_id_type=MESH)
    pl.semaphore_signal(barrier, inc=1, device_id=(me, partner), device_id_type=MESH)

    x32[...] = x_ref[...].astype(F32)
    for c in range(2):
        for q in range(tiles):
            at = (c * tiles + q) * LANES
            xs[:, at : at + LANES] = x32[pl.ds(q * 2 + c, rows, stride=2 * tiles), :].astype(BF16)

    row_ids = lax.broadcasted_iota(jnp.int32, (8, rows), 1)
    ctrl = [ctrl_ref[i] for i in range(ctrl_ref.shape[0])]
    cof = [cof_ref[i] for i in range(cof_ref.shape[0])]
    slot, rank = slot_and_rank(row_ids, rows.bit_length() - 1, target_bits, ctrl, cof)
    ahead = slot - me
    ahead = jnp.where(ahead < 0, ahead + slots, ahead)
    phase = jnp.zeros_like(rank)
    for i in range(1, phases):
        phase = phase + jnp.where(rank >= i * h, 1, 0)
    dest = phase * part_rows + ahead * h + (rank - phase * h)
    onehot = jnp.where(
        jnp.broadcast_to(dest[0:1, :], (rows, rows)) == lax.broadcasted_iota(jnp.int32, (rows, rows), 0), 1.0, 0.0
    ).astype(F32)
    picked = dot(onehot.astype(BF16), xs[...])
    for ph in range(phases):
        own[ph] = picked[ph * part_rows : (ph + 1) * part_rows, :].astype(BF16)

    pl.semaphore_wait(barrier, slots)

    swaps = []
    for ph in range(phases):
        swap = pltpu.make_async_remote_copy(
            src_ref=own.at[ph], dst_ref=part.at[ph],
            send_sem=swap_send.at[ph], recv_sem=swap_recv.at[ph],
            device_id=(me, partner), device_id_type=MESH,
        )
        swap.start()
        swaps.append(swap)

    back[...] = onehot.T.astype(BF16)
    arg_row = lax.broadcasted_iota(jnp.int32, (8, LANES), 0)
    t, f, g = ang_ref[0], ang_ref[1], ang_ref[2]
    args = jnp.where(arg_row == 0, t * 0.5, jnp.where(arg_row == 1, f, jnp.where(arg_row == 2, g, f + g)))
    cosine, sine = jnp.cos(args), jnp.sin(args)
    upper = mine >= n_narrow // 2
    coefs = coefficients([cosine[i : i + 1] for i in range(4)], [sine[i : i + 1] for i in range(4)], upper)
    for i, wc in enumerate((wc1, wc2)):
        loads[i].wait()
        wc[0:order, 0:order] = wraw[i, 0]
        wc[order:, order:] = wraw[i, 0]
        wc[0:order, order:] = wraw[i, 1]
        wc[order:, 0:order] = -wraw[i, 1]
    span = group * LANES
    p_row = lax.broadcasted_iota(jnp.int32, (span, span), 0)
    p_col = lax.broadcasted_iota(jnp.int32, (span, span), 1)
    turned = (p_row % LANES) // low * LANES + p_row // LANES * low + p_row % low
    perm[...] = jnp.where(turned == p_col, 1.0, 0.0).astype(BF16)

    goes = []
    for ph in range(phases):
        swaps[ph].wait_recv()
        for q in range(tiles):
            re = slice(q * LANES, (q + 1) * LANES)
            im = slice(order + q * LANES, order + (q + 1) * LANES)
            new_re, new_im = combine(
                coefs, own[ph, :, re].astype(F32), own[ph, :, im].astype(F32),
                part[ph, :, re].astype(F32), part[ph, :, im].astype(F32),
            )
            rot[:, re] = new_re.astype(BF16)
            rot[:, im] = new_im.astype(BF16)
        first = dot(rot[...], wc1[...])
        for k in [*range(1, slots), 0]:
            piece = jnp.concatenate(
                [first[k * h : (k + 1) * h, i * LANES : (i + 1) * LANES] for i in range(2 * tiles)], axis=0
            ).astype(BF16)
            if k == 0:
                recv[ph, me] = piece
                continue
            send[ph, k] = piece
            go = pltpu.make_async_remote_copy(
                src_ref=send.at[ph, k], dst_ref=recv.at[ph, me],
                send_sem=go_send.at[ph, k], recv_sem=go_recv.at[ph, k],
                device_id=(lax.rem(me + k, slots), mine), device_id_type=MESH,
            )
            go.start()
            goes.append((ph, go))

    returns = []
    for ph in range(phases):
        for at, go in goes:
            if at == ph:
                go.wait_recv()
        field = jnp.concatenate(
            [
                jnp.concatenate([recv[ph, v_hi * group + v_lo] for v_lo in range(group)], axis=1)
                for v_hi in range(v_his)
            ],
            axis=0,
        )
        turned_in = dot(field, perm[...]).astype(BF16)
        for mid in range(group):
            for c in range(2):
                for v_hi in range(v_his):
                    src = (v_hi * 2 + c) * qh
                    dst = (c * v_his + v_hi) * LANES
                    xmat[mid * qh : (mid + 1) * qh, dst : dst + LANES] = turned_in[
                        src : src + qh, mid * LANES : (mid + 1) * LANES
                    ]
        second = dot(xmat[...], wc2[...]).astype(BF16)
        for mid in range(group):
            for c in range(2):
                for w_hi in range(v_his):
                    dst = (w_hi * 2 + c) * qh
                    src = (c * v_his + w_hi) * LANES
                    ymat[dst : dst + qh, mid * LANES : (mid + 1) * LANES] = second[
                        mid * qh : (mid + 1) * qh, src : src + LANES
                    ]
        turned_out = dot(ymat[...], perm[...]).astype(BF16)
        for w in range(slots):
            w_hi, w_lo = w // group, w % group
            ysend[ph, w] = turned_out[w_hi * 2 * qh : (w_hi + 1) * 2 * qh, w_lo * LANES : (w_lo + 1) * LANES]
        for k in range(1, slots):
            to = lax.rem(me + k, slots)
            go = pltpu.make_async_remote_copy(
                src_ref=ysend.at[ph, to], dst_ref=ret.at[ph, slots - k],
                send_sem=ret_send.at[ph, k], recv_sem=ret_recv.at[ph, k],
                device_id=(to, mine), device_id_type=MESH,
            )
            go.start()
            returns.append((ph, go))
        ret[ph, 0] = ysend[ph, me]

    for ph in range(phases):
        for at, go in returns:
            if at == ph:
                go.wait_recv()
        came = ret[ph].astype(F32).reshape(slots, 2 * tiles, h, LANES)
        for i in range(2 * tiles):
            rmat[ph * part_rows : (ph + 1) * part_rows, i * LANES : (i + 1) * LANES] = (
                came[:, i].reshape(part_rows, LANES).astype(BF16)
            )
    final = dot(back[...], rmat[...])
    for c in range(2):
        for q in range(tiles):
            at = (c * tiles + q) * LANES
            out_ref[pl.ds(q * 2 + c, rows, stride=2 * tiles), :] = final[:, at : at + LANES]

    for swap in swaps:
        swap.wait_send()
    for _, go in goes + returns:
        go.wait_send()


def fused(dims, state, blocks_one, blocks_two, control_of, ctrl_qubits, angles):
    slots, n_narrow, order, rows, phases, low = dims
    tiles = order // LANES
    slot_rows = rows // slots
    h = slot_rows // phases
    part_rows = rows // phases
    group = LANES // low
    span = group * LANES
    piece = 2 * tiles * h
    lines = rows * tiles
    x = state.reshape(2, lines, LANES).transpose(1, 0, 2).reshape(2 * lines, LANES)
    smem = pl.BlockSpec(memory_space=pltpu.SMEM)
    vmem = pl.BlockSpec(memory_space=pltpu.VMEM)
    hbm = pl.BlockSpec(memory_space=pl.ANY)
    dma = pltpu.SemaphoreType.DMA
    out = pl.pallas_call(
        functools.partial(kernel, dims),
        out_shape=jax.ShapeDtypeStruct((2 * lines, LANES), F32),
        in_specs=[smem, smem, smem, vmem, hbm, hbm],
        out_specs=vmem,
        scratch_shapes=[
            pltpu.VMEM((2 * lines, LANES), F32),
            pltpu.VMEM((rows, 2 * order), BF16),
            pltpu.VMEM((phases, part_rows, 2 * order), BF16),
            pltpu.VMEM((phases, part_rows, 2 * order), BF16),
            pltpu.VMEM((part_rows, 2 * order), BF16),
            pltpu.VMEM((2, 2, order, order), BF16),
            pltpu.VMEM((2 * order, 2 * order), BF16),
            pltpu.VMEM((2 * order, 2 * order), BF16),
            pltpu.VMEM((span, span), BF16),
            pltpu.VMEM((rows, rows), BF16),
            pltpu.VMEM((phases, slots, piece, LANES), BF16),
            pltpu.VMEM((phases, slots, piece, LANES), BF16),
            pltpu.VMEM((group * tiles * h, 2 * order), BF16),
            pltpu.VMEM((slots // group * piece, span), BF16),
            pltpu.VMEM((phases, slots, piece, LANES), BF16),
            pltpu.VMEM((phases, slots, piece, LANES), BF16),
            pltpu.VMEM((rows, 2 * order), BF16),
            dma((2,)),
            dma((phases,)),
            dma((phases,)),
            dma((phases, slots)),
            dma((phases, slots)),
            dma((phases, slots)),
            dma((phases, slots)),
        ],
        compiler_params=pltpu.CompilerParams(
            collective_id=0, has_side_effects=True, vmem_limit_bytes=40 * 2**20
        ),
    )(ctrl_qubits, control_of, angles, x, blocks_one, blocks_two)
    return out.reshape(lines, 2, LANES).transpose(1, 0, 2).reshape(2, lines * LANES)


def complex_dot(spec, field, weights):
    products = jnp.einsum(spec, field, weights, preferred_element_type=F32)
    return jnp.stack([products[0, 0] - products[1, 1], products[0, 1] + products[1, 0]])


def plain(dims, state, blocks_one, blocks_two, control_of, ctrl_qubits, angles):
    slots, n_narrow, order, rows, _, low = dims
    slot_rows = rows // slots
    mids = order // low
    mine = lax.axis_index("narrow")
    half = n_narrow // 2
    pairs = [(source, (source + half) % n_narrow) for source in range(n_narrow)]
    far = lax.ppermute(state, "narrow", pairs).astype(F32)
    near = state.astype(F32)
    args = [angles[0] * 0.5, angles[1], angles[2], angles[1] + angles[2]]
    coefs = coefficients([jnp.cos(a) for a in args], [jnp.sin(a) for a in args], mine >= half)
    rotated = jnp.stack(combine(coefs, near[0], near[1], far[0], far[1])).astype(BF16)
    row_ids = jnp.arange(rows, dtype=jnp.int32)
    ctrl = [ctrl_qubits[i] for i in range(ctrl_qubits.shape[0])]
    cof = [control_of[i] for i in range(control_of.shape[0])]
    slot, rank = slot_and_rank(row_ids, rows.bit_length() - 1, order.bit_length() - 1, ctrl, cof)
    dest = slot * slot_rows + rank
    onehot = (dest[None, :] == row_ids[:, None]).astype(BF16)
    first = complex_dot("crs,dst->cdrt", rotated.reshape(2, rows, order), blocks_one[0]).astype(BF16)
    picked = jnp.einsum("pr,crt->cpt", onehot, first, preferred_element_type=F32).astype(BF16)
    picked = picked.reshape(2, slots, slot_rows, mids, low)
    arranged = jnp.transpose(picked, (0, 1, 4, 2, 3)).reshape(2, slots, low, rows)
    received = lax.all_to_all(arranged, "wide", split_axis=1, concat_axis=2, tiled=True)
    mixed = complex_dot("cth,dtu->cduh", received[:, 0], blocks_two[0]).astype(BF16)[:, None]
    returned = lax.all_to_all(mixed, "wide", split_axis=2, concat_axis=1, tiled=True)
    returned = returned.reshape(2, slots, low, slot_rows, mids)
    returned = jnp.transpose(returned, (0, 1, 3, 4, 2)).reshape(2, rows, order)
    final = jnp.einsum("pr,cpt->crt", onehot, returned, preferred_element_type=F32)
    return final.reshape(2, rows * order)


def shards(*operands):
    state, blocks_one = operands[:2]
    slots = lax.axis_size("wide")
    order = blocks_one.shape[2]
    rows = state.shape[1] // order
    low = order // slots
    slot_rows = rows // slots
    phases = 2 if slot_rows % 16 == 0 else 1
    dims = (slots, lax.axis_size("narrow"), order, rows, phases, low)
    fits = slot_rows % 8 == 0 and LANES % low == 0 and slots % (LANES // low) == 0
    return (fused if fits else plain)(dims, *operands)


def solution(mesh):
    in_specs = (
        P(None, ("wide", "narrow")),
        P("wide", None, None, None),
        P("wide", None, None, None),
        P(),
        P(),
        P(),
    )
    out_specs = P(None, ("wide", "narrow"))
    return jax.shard_map(shards, mesh=mesh, in_specs=in_specs, out_specs=out_specs, check_vma=False)
```

time: 126 us -> 43.9 us (0.35)
  blocking collectives: 49.1 us -> 0 us
  Pallas kernels: 0 us -> 38.5 us
  local copies, waits for them, and re-layouts: 34.4 us -> 5.15 us
  other arithmetic: 26.2 us -> 0 us
  between operations: 10.4 us -> 0.02 us
  starting transfers between devices: 2.94 us -> 0 us
  matrix products: 1.43 us -> 0 us
    all_to_all x2 -> x0, blocking collectives: 49.1 us -> none  [the longest x1 28.9 us: send_back(): lax.all_to_all(mixed, 'wide', split_axis=2, concat_axis=1, tiled=True)]
    pallas_call x0 -> x1, Pallas kernels: none -> 38.5 us  [fused(): pl.pallas_call(functools.partial(kernel, dims), out_shape=jax.ShapeDtypeS...]
    and x6 -> x0, other arithmetic: 10.7 us -> none  [the longest x1 5.66 us: slot_index(): from_control = jnp.right_shift(values, control_place[qubit]) & 1]
    reshape x4 -> x0, local copies, waits for them, and re-layouts: 8.81 us -> none  [the longest x2 4.36 us: shards(): jnp.transpose(back_rows, (0, 1, 3, 4, 2)).reshape(2, high_count, order)]
    scatter x1 -> x0, local copies, waits for them, and re-layouts: 6.93 us -> none  [shards(): jnp.zeros((2, high_count, order), jnp.float32).at[:, row_ids].set(back_rows)]
    another operation x3 -> x0, other arithmetic: 5.79 us -> none
    gather x2 -> x0, local copies, waits for them, and re-layouts: 5.47 us -> none  [shards(): jnp.take(first, row_ids, axis=1)]
    transpose x1 -> x0, local copies, waits for them, and re-layouts: 5.4 us -> none  [shards(): jnp.transpose(back_rows, (0, 1, 3, 4, 2)).reshape(2, high_count, order)]
  transfers between devices with their start and end apart: 1 -> 0, of which waited for: 0 -> 0; matrix products, arithmetic and copies ran while one was open for 18% -> 0% of each run, Pallas kernels for 0% -> 0%
where the time goes in v1:
time: 43.9 us; the launch traced here: 43.6 us
  Pallas kernels  38.5 us (88%)
  local copies, waits for them, and re-layouts  5.15 us (12%)
    pallas_call x1, Pallas kernels, fused(): pl.pallas_call(functools.partial(kernel, dims), out_shape=jax.ShapeDtypeS...  38.5 us
    unnamed x13, local copies, waits for them, and re-layouts  5.15 us

profile of v1, /device:TPU:0, one launch (start us, length us, event | category | flops | bytes accessed | tf_op | source)
XLA Modules:
  0.0 43.6 jit_solution(5354405307228327063)
XLA Ops:
  0.0 0.0 copy-start.5
  0.0 0.0 copy-start.3
  0.0 0.0 copy-start.4
  0.0 0.6 %copy-done.5 = f32[3]{0:T(128)S(1)} copy-done((f32[3]{0:T(128)S(1)}, f32[3]{0:T(128)}, u32[]{:S(2)}) %copy-start.5) | copy-done | bytes 36
  0.7 0.0 copy-done.3
  0.7 0.0 copy-done.4
  0.7 0.0 copy-start
  0.7 1.2 %copy-done = bf16[1,2,512,512]{3,2,1,0:T(8,128)(2,1)S(1)} copy-done((bf16[1,2,512,512]{3,2,1,0:T(8,128)(2,1)S(1)}, bf16[1,2,512,512]{3,2,1,0:T(8,128)(2,1)}, u32[]{:S(2)}) %copy-start) | copy-done | bytes 1048600
  1.9 0.0 copy-start.1
  1.9 1.2 %copy-done.1 = bf16[1,2,512,512]{3,2,1,0:T(8,128)(2,1)S(1)} copy-done((bf16[1,2,512,512]{3,2,1,0:T(8,128)(2,1)S(1)}, bf16[1,2,512,512]{3,2,1,0:T(8,128)(2,1)}, u32[]{:S(2)}) %copy-start.1) | copy-done | bytes 1048600
  3.1 0.0 copy-start.2
  3.1 1.0 %copy-done.2 = bf16[2,131072]{1,0:T(2,128)(2,1)S(1)} copy-done((bf16[2,131072]{1,0:T(2,128)(2,1)S(1)}, bf16[2,131072]{1,0:T(2,128)(2,1)}, u32[]{:S(2)}) %copy-start.2) | copy-done | bytes 524312
  4.2 38.5 %shard_map.64 = f32[2048,128]{1,0:T(8,128)S(1)} custom-call(s32[4]{0:T(128)S(1)} %copy-done.3, s32[16]{0:T(128)S(1)} %copy-done.4, f32[3]{0:T(128)S(1)} %copy-done.5, bf16[2048,128]{1,0:T(8,128)(2,1)S(1)} %bitcast.11, bf16[1,2,512,512]{3,2,1,0:T(8,128)(2,1)S(1)} %copy-done, bf16[1,2,512,512]{3,2,1,0:T(8,128)(2,1)S(1)} %copy-done.1), custom_call_target="tpu_custom_call" | custom-call | tf_op jit(solution)/shard_map/pallas_call | solution.py:254
  42.6 1.0 %copy.10 = f32[2,131072]{1,0:T(2,128)} copy(f32[2,131072]{1,0:T(2,128)S(1)} %bitcast.10) | data formatting | bytes 2097152
Async XLA Ops:
  0.0 0.7 %copy-start.5 = (f32[3]{0:T(128)S(1)}, f32[3]{0:T(128)}, u32[]{:S(2)}) copy-start(f32[3]{0:T(128)} %ang_ref.1) | copy-start | bytes 40
  0.0 0.7 %copy-start.3 = (s32[4]{0:T(128)S(1)}, s32[4]{0:T(128)}, u32[]{:S(2)}) copy-start(s32[4]{0:T(128)} %ctrl_ref.1) | copy-start | bytes 52
  0.0 0.7 %copy-start.4 = (s32[16]{0:T(128)S(1)}, s32[16]{0:T(128)}, u32[]{:S(2)}) copy-start(s32[16]{0:T(128)} %cof_ref.1) | copy-start | bytes 196
  0.7 1.2 %copy-start = (bf16[1,2,512,512]{3,2,1,0:T(8,128)(2,1)S(1)}, bf16[1,2,512,512]{3,2,1,0:T(8,128)(2,1)}, u32[]{:S(2)}) copy-start(bf16[1,2,512,512]{3,2,1,0:T(8,128)(2,1)} %w1_ref.1) | copy-start | bytes 3145732
  1.9 1.2 %copy-start.1 = (bf16[1,2,512,512]{3,2,1,0:T(8,128)(2,1)S(1)}, bf16[1,2,512,512]{3,2,1,0:T(8,128)(2,1)}, u32[]{:S(2)}) copy-start(bf16[1,2,512,512]{3,2,1,0:T(8,128)(2,1)} %w2_ref.1) | copy-start | bytes 3145732
  3.1 1.0 %copy-start.2 = (bf16[2,131072]{1,0:T(2,128)(2,1)S(1)}, bf16[2,131072]{1,0:T(2,128)(2,1)}, u32[]{:S(2)}) copy-start(bf16[2,131072]{1,0:T(2,128)(2,1)} %param.6) | copy-start | bytes 1572868

commit v2 on v1

--- a/solution.py
+++ b/solution.py
@@ -8,6 +8,8 @@
 from jax.sharding import PartitionSpec as P
 
 LANES = 128
+LANE_BITS = 7
+CUTS = 4
 F32 = jnp.float32
 BF16 = jnp.bfloat16
 MESH = pl.DeviceIdType.MESH
@@ -38,6 +40,11 @@
     return slot, rank
 
 
+def visit_order(slots):
+    half = slots // 2
+    return [half + i // 2 if i % 2 == 0 else half - 1 - i // 2 for i in range(slots)]
+
+
 def coefficients(cosine, sine, upper):
     own_re = jnp.where(upper, cosine[3] * cosine[0], cosine[0])
     own_im = jnp.where(upper, sine[3] * cosine[0], jnp.zeros_like(sine[3]))
@@ -58,7 +65,7 @@
     dims,
     ctrl_ref, cof_ref, ang_ref, x_ref, w1_ref, w2_ref,
     out_ref,
-    x32, xs, own, part, rot, wraw, wc1, wc2, perm, back,
+    xraw, x32, xs, own, part, rot, wraw, wc1, wc2, perm, back,
     send, recv, xmat, ymat, ysend, ret, rmat,
     load_sem, swap_send, swap_recv, go_send, go_recv, ret_send, ret_recv,
 ):
@@ -73,13 +80,15 @@
     target_bits = order.bit_length() - 1
     me = lax.axis_index("wide")
     mine = lax.axis_index("narrow")
+    order_of = visit_order(slots)
     partner = lax.rem(mine + n_narrow // 2, n_narrow)
 
     loads = [
         pltpu.make_async_copy(w_ref.at[0], wraw.at[i], load_sem.at[i])
         for i, w_ref in enumerate((w1_ref, w2_ref))
     ]
-    for load in loads:
+    fetch = pltpu.make_async_copy(x_ref, xraw, load_sem.at[2])
+    for load in [fetch, *loads]:
         load.start()
 
     barrier = pltpu.get_barrier_semaphore()
@@ -87,7 +96,8 @@
         pl.semaphore_signal(barrier, inc=1, device_id=(lax.rem(me + k, slots), mine), device_id_type=MESH)
     pl.semaphore_signal(barrier, inc=1, device_id=(me, partner), device_id_type=MESH)
 
-    x32[...] = x_ref[...].astype(F32)
+    fetch.wait()
+    x32[...] = xraw[...].astype(F32)
     for c in range(2):
         for q in range(tiles):
             at = (c * tiles + q) * LANES
@@ -102,25 +112,32 @@
     phase = jnp.zeros_like(rank)
     for i in range(1, phases):
         phase = phase + jnp.where(rank >= i * h, 1, 0)
-    dest = phase * part_rows + ahead * h + (rank - phase * h)
+    half = slots // 2
+    place = jnp.where(ahead >= half, 2 * (ahead - half), 2 * (half - ahead) - 1)
+    dest = phase * part_rows + place * h + (rank - phase * h)
     onehot = jnp.where(
         jnp.broadcast_to(dest[0:1, :], (rows, rows)) == lax.broadcasted_iota(jnp.int32, (rows, rows), 0), 1.0, 0.0
     ).astype(F32)
     picked = dot(onehot.astype(BF16), xs[...])
     for ph in range(phases):
-        own[ph] = picked[ph * part_rows : (ph + 1) * part_rows, :].astype(BF16)
+        for cut in range(own.shape[1]):
+            at = (ph * own.shape[1] + cut) * own.shape[2]
+            own[ph, cut] = picked[at : at + own.shape[2], :].astype(BF16)
 
     pl.semaphore_wait(barrier, slots)
 
+    cuts = CUTS
+    per_cut = slots // cuts
     swaps = []
     for ph in range(phases):
-        swap = pltpu.make_async_remote_copy(
-            src_ref=own.at[ph], dst_ref=part.at[ph],
-            send_sem=swap_send.at[ph], recv_sem=swap_recv.at[ph],
-            device_id=(me, partner), device_id_type=MESH,
-        )
-        swap.start()
-        swaps.append(swap)
+        for cut in range(cuts):
+            swap = pltpu.make_async_remote_copy(
+                src_ref=own.at[ph, cut], dst_ref=part.at[ph, cut],
+                send_sem=swap_send.at[ph, cut], recv_sem=swap_recv.at[ph, cut],
+                device_id=(me, partner), device_id_type=MESH,
+            )
+            swap.start()
+            swaps.append(swap)
 
     back[...] = onehot.T.astype(BF16)
     arg_row = lax.broadcasted_iota(jnp.int32, (8, LANES), 0)
@@ -138,37 +155,40 @@
     span = group * LANES
     p_row = lax.broadcasted_iota(jnp.int32, (span, span), 0)
     p_col = lax.broadcasted_iota(jnp.int32, (span, span), 1)
-    turned = (p_row % LANES) // low * LANES + p_row // LANES * low + p_row % low
+    low_bits = low.bit_length() - 1
+    turned = ((p_row & (LANES - 1)) >> low_bits) * LANES + (p_row >> LANE_BITS) * low + (p_row & (low - 1))
     perm[...] = jnp.where(turned == p_col, 1.0, 0.0).astype(BF16)
 
     goes = []
     for ph in range(phases):
-        swaps[ph].wait_recv()
-        for q in range(tiles):
-            re = slice(q * LANES, (q + 1) * LANES)
-            im = slice(order + q * LANES, order + (q + 1) * LANES)
-            new_re, new_im = combine(
-                coefs, own[ph, :, re].astype(F32), own[ph, :, im].astype(F32),
-                part[ph, :, re].astype(F32), part[ph, :, im].astype(F32),
-            )
-            rot[:, re] = new_re.astype(BF16)
-            rot[:, im] = new_im.astype(BF16)
-        first = dot(rot[...], wc1[...])
-        for k in [*range(1, slots), 0]:
-            piece = jnp.concatenate(
-                [first[k * h : (k + 1) * h, i * LANES : (i + 1) * LANES] for i in range(2 * tiles)], axis=0
-            ).astype(BF16)
-            if k == 0:
-                recv[ph, me] = piece
-                continue
-            send[ph, k] = piece
-            go = pltpu.make_async_remote_copy(
-                src_ref=send.at[ph, k], dst_ref=recv.at[ph, me],
-                send_sem=go_send.at[ph, k], recv_sem=go_recv.at[ph, k],
-                device_id=(lax.rem(me + k, slots), mine), device_id_type=MESH,
-            )
-            go.start()
-            goes.append((ph, go))
+        for cut in range(cuts):
+            swaps[ph * cuts + cut].wait_recv()
+            for q in range(tiles):
+                re = slice(q * LANES, (q + 1) * LANES)
+                im = slice(order + q * LANES, order + (q + 1) * LANES)
+                new_re, new_im = combine(
+                    coefs, own[ph, cut, :, re].astype(F32), own[ph, cut, :, im].astype(F32),
+                    part[ph, cut, :, re].astype(F32), part[ph, cut, :, im].astype(F32),
+                )
+                rot[:, re] = new_re.astype(BF16)
+                rot[:, im] = new_im.astype(BF16)
+            first = dot(rot[...], wc1[...])
+            for i in range(per_cut):
+                k = order_of[cut * per_cut + i]
+                piece = jnp.concatenate(
+                    [first[i * h : (i + 1) * h, j * LANES : (j + 1) * LANES] for j in range(2 * tiles)], axis=0
+                ).astype(BF16)
+                if k == 0:
+                    recv[ph, me] = piece
+                    continue
+                send[ph, k] = piece
+                go = pltpu.make_async_remote_copy(
+                    src_ref=send.at[ph, k], dst_ref=recv.at[ph, me],
+                    send_sem=go_send.at[ph, k], recv_sem=go_recv.at[ph, k],
+                    device_id=(lax.rem(me + k, slots), mine), device_id_type=MESH,
+                )
+                go.start()
+                goes.append((ph, go))
 
     returns = []
     for ph in range(phases):
@@ -204,27 +224,27 @@
         for w in range(slots):
             w_hi, w_lo = w // group, w % group
             ysend[ph, w] = turned_out[w_hi * 2 * qh : (w_hi + 1) * 2 * qh, w_lo * LANES : (w_lo + 1) * LANES]
-        for k in range(1, slots):
+        for k in order_of[:-1]:
             to = lax.rem(me + k, slots)
             go = pltpu.make_async_remote_copy(
-                src_ref=ysend.at[ph, to], dst_ref=ret.at[ph, slots - k],
+                src_ref=ysend.at[ph, to], dst_ref=ret.at[ph, order_of.index(slots - k)],
                 send_sem=ret_send.at[ph, k], recv_sem=ret_recv.at[ph, k],
                 device_id=(to, mine), device_id_type=MESH,
             )
             go.start()
             returns.append((ph, go))
-        ret[ph, 0] = ysend[ph, me]
-
+        ret[ph, slots - 1] = ysend[ph, me]
+
+    final = None
     for ph in range(phases):
         for at, go in returns:
             if at == ph:
                 go.wait_recv()
         came = ret[ph].astype(F32).reshape(slots, 2 * tiles, h, LANES)
         for i in range(2 * tiles):
-            rmat[ph * part_rows : (ph + 1) * part_rows, i * LANES : (i + 1) * LANES] = (
-                came[:, i].reshape(part_rows, LANES).astype(BF16)
-            )
-    final = dot(back[...], rmat[...])
+            rmat[:, i * LANES : (i + 1) * LANES] = came[:, i].reshape(part_rows, LANES).astype(BF16)
+        add = dot(back[:, ph * part_rows : (ph + 1) * part_rows], rmat[...])
+        final = add if final is None else final + add
     for c in range(2):
         for q in range(tiles):
             at = (c * tiles + q) * LANES
@@ -245,6 +265,7 @@
     group = LANES // low
     span = group * LANES
     piece = 2 * tiles * h
+    cuts = CUTS
     lines = rows * tiles
     x = state.reshape(2, lines, LANES).transpose(1, 0, 2).reshape(2 * lines, LANES)
     smem = pl.BlockSpec(memory_space=pltpu.SMEM)
@@ -254,14 +275,15 @@
     out = pl.pallas_call(
         functools.partial(kernel, dims),
         out_shape=jax.ShapeDtypeStruct((2 * lines, LANES), F32),
-        in_specs=[smem, smem, smem, vmem, hbm, hbm],
+        in_specs=[smem, smem, smem, hbm, hbm, hbm],
         out_specs=vmem,
         scratch_shapes=[
+            pltpu.VMEM((2 * lines, LANES), BF16),
             pltpu.VMEM((2 * lines, LANES), F32),
             pltpu.VMEM((rows, 2 * order), BF16),
-            pltpu.VMEM((phases, part_rows, 2 * order), BF16),
-            pltpu.VMEM((phases, part_rows, 2 * order), BF16),
-            pltpu.VMEM((part_rows, 2 * order), BF16),
+            pltpu.VMEM((phases, cuts, part_rows // cuts, 2 * order), BF16),
+            pltpu.VMEM((phases, cuts, part_rows // cuts, 2 * order), BF16),
+            pltpu.VMEM((part_rows // cuts, 2 * order), BF16),
             pltpu.VMEM((2, 2, order, order), BF16),
             pltpu.VMEM((2 * order, 2 * order), BF16),
             pltpu.VMEM((2 * order, 2 * order), BF16),
@@ -273,17 +295,17 @@
             pltpu.VMEM((slots // group * piece, span), BF16),
             pltpu.VMEM((phases, slots, piece, LANES), BF16),
             pltpu.VMEM((phases, slots, piece, LANES), BF16),
-            pltpu.VMEM((rows, 2 * order), BF16),
-            dma((2,)),
-            dma((phases,)),
-            dma((phases,)),
+            pltpu.VMEM((part_rows, 2 * order), BF16),
+            dma((3,)),
+            dma((phases, cuts)),
+            dma((phases, cuts)),
             dma((phases, slots)),
             dma((phases, slots)),
             dma((phases, slots)),
             dma((phases, slots)),
         ],
         compiler_params=pltpu.CompilerParams(
-            collective_id=0, has_side_effects=True, vmem_limit_bytes=40 * 2**20
+            collective_id=0, has_side_effects=True, vmem_limit_bytes=60 * 2**20
         ),
     )(ctrl_qubits, control_of, angles, x, blocks_one, blocks_two)
     return out.reshape(lines, 2, LANES).transpose(1, 0, 2).reshape(2, lines * LANES)
@@ -334,7 +356,7 @@
     slot_rows = rows // slots
     phases = 2 if slot_rows % 16 == 0 else 1
     dims = (slots, lax.axis_size("narrow"), order, rows, phases, low)
-    fits = slot_rows % 8 == 0 and LANES % low == 0 and slots % (LANES // low) == 0
+    fits = slot_rows % 8 == 0 and slots % CUTS == 0 and LANES % low == 0 and slots % (LANES // low) == 0
     return (fused if fits else plain)(dims, *operands)
 
 

time: 43.9 us -> 39.3 us (0.90)
  local copies, waits for them, and re-layouts: 5.15 us -> 2.26 us
  Pallas kernels: 38.5 us -> 36.8 us
    unnamed x13 -> x1, local copies, waits for them, and re-layouts: 5.15 us -> 2.26 us
    pallas_call x1, Pallas kernels: 38.5 us -> 36.8 us  [fused(): pl.pallas_call(functools.partial(kernel, dims), out_shape=jax.ShapeDtypeS...]
where the time goes in v2:
time: 39.3 us; the launch traced here: 39.1 us
  Pallas kernels  36.8 us (94%)
  local copies, waits for them, and re-layouts  2.26 us (6%)
    pallas_call x1, Pallas kernels, fused(): pl.pallas_call(functools.partial(kernel, dims), out_shape=jax.ShapeDtypeS...  36.8 us
    unnamed x1, local copies, waits for them, and re-layouts  2.26 us

profile of v2, /device:TPU:0, one launch (start us, length us, event | category | flops | bytes accessed | tf_op | source)
XLA Modules:
  0.0 39.1 jit_solution(15231274585752481083)
XLA Ops:
  0.0 36.8 %shard_map.64 = f32[2048,128]{1,0:T(8,128)} custom-call(s32[4]{0:T(128)} %ctrl_ref.1, s32[16]{0:T(128)} %cof_ref.1, f32[3]{0:T(128)} %ang_ref.1, bf16[2048,128]{1,0:T(8,128)(2,1)} %bitcast.11, bf16[1,2,512,512]{3,2,1,0:T(8,128)(2,1)} %w1_ref.1, bf16[1,2,512,512]{3,2,1,0:T(8,128)(2,1)} %w2_ref.1), custom_call_target="tpu_custom_call" | custom-call | tf_op jit(solution)/shard_map/pallas_call | solution.py:275
  36.9 2.3 %copy.10 = f32[2,131072]{1,0:T(2,128)} copy(f32[2,131072]{1,0:T(2,128)} %bitcast.10) | data formatting | bytes 2097152

commit v3 on v2

--- a/solution.py
+++ b/solution.py
@@ -305,7 +305,7 @@
             dma((phases, slots)),
         ],
         compiler_params=pltpu.CompilerParams(
-            collective_id=0, has_side_effects=True, vmem_limit_bytes=60 * 2**20
+            collective_id=0, has_side_effects=True, vmem_limit_bytes=52 * 2**20
         ),
     )(ctrl_qubits, control_of, angles, x, blocks_one, blocks_two)
     return out.reshape(lines, 2, LANES).transpose(1, 0, 2).reshape(2, lines * LANES)

time: 39.3 us -> 38.6 us (0.982)
  Pallas kernels: 36.8 us -> 35.8 us
  local copies, waits for them, and re-layouts: 2.26 us -> 2.7 us
    pallas_call x1, Pallas kernels: 36.8 us -> 35.8 us  [fused(): pl.pallas_call(functools.partial(kernel, dims), out_shape=jax.ShapeDtypeS...]
    unnamed x1 -> x9, local copies, waits for them, and re-layouts: 2.26 us -> 2.7 us
where the time goes in v3:
time: 38.6 us; the launch traced here: 38.5 us
  Pallas kernels  35.8 us (93%)
  local copies, waits for them, and re-layouts  2.7 us (7%)
    pallas_call x1, Pallas kernels, fused(): pl.pallas_call(functools.partial(kernel, dims), out_shape=jax.ShapeDtypeS...  35.8 us
    unnamed x9, local copies, waits for them, and re-layouts  2.7 us

profile of v3, /device:TPU:0, one launch (start us, length us, event | category | flops | bytes accessed | tf_op | source)
XLA Modules:
  0.0 38.5 jit_solution(16678066982025473327)
XLA Ops:
  0.0 0.0 copy-start.3
  0.0 0.0 copy-start.1
  0.0 0.0 copy-start.2
  0.0 0.6 %copy-done.3 = f32[3]{0:T(128)S(1)} copy-done((f32[3]{0:T(128)S(1)}, f32[3]{0:T(128)}, u32[]{:S(2)}) %copy-start.3) | copy-done | bytes 36
  0.7 0.0 copy-done.1
  0.7 0.0 copy-done.2
  0.7 0.0 copy-start
  0.7 1.0 %copy-done = bf16[2,131072]{1,0:T(2,128)(2,1)S(1)} copy-done((bf16[2,131072]{1,0:T(2,128)(2,1)S(1)}, bf16[2,131072]{1,0:T(2,128)(2,1)}, u32[]{:S(2)}) %copy-start) | copy-done | bytes 524312
  1.7 35.8 %shard_map.64 = f32[2048,128]{1,0:T(8,128)S(1)} custom-call(s32[4]{0:T(128)S(1)} %copy-done.1, s32[16]{0:T(128)S(1)} %copy-done.2, f32[3]{0:T(128)S(1)} %copy-done.3, bf16[2048,128]{1,0:T(8,128)(2,1)S(1)} %bitcast.11, bf16[1,2,512,512]{3,2,1,0:T(8,128)(2,1)} %w1_ref.1, bf16[1,2,512,512]{3,2,1,0:T(8,128)(2,1)} %w2_ref.1), custom_call_target="tpu_custom_call" | custom-call | tf_op jit(solution)/shard_map/pallas_call | solution.py:275
  37.5 1.0 %copy.10 = f32[2,131072]{1,0:T(2,128)} copy(f32[2,131072]{1,0:T(2,128)S(1)} %bitcast.10) | data formatting | bytes 2097152
Async XLA Ops:
  0.0 0.7 %copy-start.3 = (f32[3]{0:T(128)S(1)}, f32[3]{0:T(128)}, u32[]{:S(2)}) copy-start(f32[3]{0:T(128)} %ang_ref.1) | copy-start | bytes 40
  0.0 0.7 %copy-start.1 = (s32[4]{0:T(128)S(1)}, s32[4]{0:T(128)}, u32[]{:S(2)}) copy-start(s32[4]{0:T(128)} %ctrl_ref.1) | copy-start | bytes 52
  0.0 0.7 %copy-start.2 = (s32[16]{0:T(128)S(1)}, s32[16]{0:T(128)}, u32[]{:S(2)}) copy-start(s32[16]{0:T(128)} %cof_ref.1) | copy-start | bytes 196
  0.7 1.0 %copy-start = (bf16[2,131072]{1,0:T(2,128)(2,1)S(1)}, bf16[2,131072]{1,0:T(2,128)(2,1)}, u32[]{:S(2)}) copy-start(bf16[2,131072]{1,0:T(2,128)(2,1)} %param.6) | copy-start | bytes 1572868
